TPU v7x, 32 devices: a whole 2x2x4 slice. The times are simulated.
32 devices in a mesh: gx: 4 (over z), gy: 4 (over y, x), gz: 2 (over core).
Axes of the slice: x: 2, y: 2, z: 4, core: 2. Of those that a mesh axis runs over, the one named last changes fastest.
Arguments:
- volt: float32 [32, 128, 512], P('gz', 'gx', 'gy'), may hold values from 0 to 1
- recovery: float32 [32, 128, 512], P('gz', 'gx', 'gy'), may hold values from 0 to 1
- fiber_class: int32 [32, 128, 512], P('gz', 'gx', 'gy'), may hold values from 0 to 7
- fiber_table: float32 [3, 8], replicated, may hold values from 0.02 to 0.16
- junction_block: int32 [4096], P(('gx', 'gy', 'gz')), may hold values from 0 to 511
- junction_term: int32 [4096], P(('gx', 'gy', 'gz')), may hold values from 0 to 31
- junction_owner: int32 [4096, 1], P(('gx', 'gy', 'gz')), may hold values from 0 to 15; in each aligned block of 128 rows (0 to 127, 128 to 255, ...) at most 16 rows name the same one
- term_volt: float32 [1024, 128], P(('gx', 'gy', 'gz')), may hold values from 0 to 1
- term_recovery: float32 [1024, 128], P(('gx', 'gy', 'gz')), may hold values from 0 to 1
- term_gain: float32 [1024], P(('gx', 'gy', 'gz')), may hold values from 0.5 to 4
- cable_gain: float32 [1024], P(('gx', 'gy', 'gz')), may hold values from 0.05 to 0.45
Outputs:
- volt_out: float32 [32, 128, 512], P('gz', 'gx', 'gy')
- recovery_out: float32 [32, 128, 512], P('gz', 'gx', 'gy')
- term_volt_out: float32 [1024, 128], P(('gx', 'gy', 'gz'))
- term_recovery_out: float32 [1024, 128], P(('gx', 'gy', 'gz'))
Inputs may be any that keep to these rules, and one draw needn't show every extreme that they name: `junction_owner`: among the 128 junctions of one device, at most 16 have the same owner, a bound that some block reaches.
All inputs are finite; a program needn't handle non-finite values.
Results may differ from a plain program's by a relative error of at most 0.00002.
Values sent between devices are 32-bit elements; how exact they have to be, the bound alone decides.
A program may use at most 64 MiB of HBM per device.

v0:
```python
import jax
import jax.numpy as jnp
from jax import lax
from jax.sharding import PartitionSpec as P

NCLASS = 8
STEPS = 4


def extended(cells, sides, width):
    for axis, dim in sides:
        count = lax.axis_size(axis)
        ends = count - 1
        head = lax.slice_in_dim(cells, 0, width, axis=dim)
        tail = lax.slice_in_dim(cells, cells.shape[dim] - width, cells.shape[dim], axis=dim)
        cells = jnp.concatenate(
            [
                lax.ppermute(tail, axis, [(i, (i + 1) % count) for i in range(ends)]),
                cells,
                lax.ppermute(head, axis, [((i + 1) % count, i) for i in range(ends)]),
            ],
            axis=dim,
        )
    return cells


def cell_kinetics(v, w, drive):
    react = -8.0 * v * (v - 0.15) * (v - 1.0) - v * w
    new_v = 0.1 * (react + drive)
    new_w = w + 0.01 * (-w - 8.0 * v * (v - 1.15))
    return (new_v, new_w)


def edge_fix(padded, dim, at_low, at_high):
    count = padded.shape[dim]
    lower = lax.slice_in_dim(padded, 0, 1, axis=dim)
    lower_in = lax.slice_in_dim(padded, 1, 2, axis=dim)
    upper = lax.slice_in_dim(padded, count - 1, count, axis=dim)
    upper_in = lax.slice_in_dim(padded, count - 2, count - 1, axis=dim)
    middle = lax.slice_in_dim(padded, 1, count - 1, axis=dim)
    lower = jnp.where(at_low, lower_in, lower)
    upper = jnp.where(at_high, upper_in, upper)
    return jnp.concatenate([lower, middle, upper], axis=dim)


def on_device(
    volt,
    recovery,
    fiber_class,
    fiber_table,
    junction_block,
    junction_term,
    junction_owner,
    term_volt,
    term_recovery,
    term_gain,
    cable_gain,
):
    depth, rows_x, width = volt.shape
    n_gx = lax.axis_size("gx")
    owners = n_gx * lax.axis_size("gy")
    jcount = junction_block.shape[0]
    capacity = max(2, 2 * jcount // owners)
    slots_total = owners * capacity
    term_count = term_volt.shape[0]
    low_z = lax.axis_index("gz") == 0
    high_z = lax.axis_index("gz") == lax.axis_size("gz") - 1
    low_x = lax.axis_index("gx") == 0
    high_x = lax.axis_index("gx") == lax.axis_size("gx") - 1
    low_y = lax.axis_index("gy") == 0
    high_y = lax.axis_index("gy") == lax.axis_size("gy") - 1
    coef_z = jnp.zeros(volt.shape, jnp.float32)
    coef_x = jnp.zeros(volt.shape, jnp.float32)
    coef_y = jnp.zeros(volt.shape, jnp.float32)
    for klass in range(NCLASS):
        hit = fiber_class == klass
        coef_z = jnp.where(hit, fiber_table[0, klass], coef_z)
        coef_x = jnp.where(hit, fiber_table[1, klass], coef_x)
        coef_y = jnp.where(hit, fiber_table[2, klass], coef_y)
    owner = junction_owner[:, 0]
    order = jnp.arange(jcount, dtype=jnp.int32)
    earlier = (owner[:, None] == owner[None, :]) & (order[None, :] < order[:, None])
    rank = jnp.sum(earlier.astype(jnp.int32), axis=1)
    slot = owner * capacity + rank
    id_buffer = jnp.full((slots_total,), -1, jnp.int32).at[slot].set(junction_term)
    arrived = lax.all_to_all(id_buffer, ("gx", "gy"), split_axis=0, concat_axis=0, tiled=True)
    valid = arrived >= 0
    safe_ids = jnp.where(valid, arrived, 0)
    gains = jnp.where(valid, term_gain[safe_ids], 0.0)
    for step in range(STEPS):
        flat_rows = volt.reshape(depth * rows_x, width)
        sent = jnp.zeros((slots_total, width), jnp.float32).at[slot].set(flat_rows[junction_block])
        far_volt = term_volt[safe_ids]
        received = lax.all_to_all(sent, ("gx", "gy"), split_axis=0, concat_axis=0, tiled=True)
        current = gains[:, None] * (far_volt - received)
        returned = lax.all_to_all(current, ("gx", "gy"), split_axis=0, concat_axis=0, tiled=True)
        into_voxel = jax.ops.segment_sum(
            returned[slot], junction_block, num_segments=depth * rows_x
        ).reshape(depth, rows_x, width)
        into_term = jax.ops.segment_sum(-current, safe_ids, num_segments=term_count)
        padded = extended(volt, (("gx", 1), ("gy", 2), ("gz", 0)), 1)
        padded = edge_fix(padded, 0, low_z, high_z)
        padded = edge_fix(padded, 1, low_x, high_x)
        padded = edge_fix(padded, 2, low_y, high_y)
        lap_z = padded[2:, 1:-1, 1:-1] + padded[:-2, 1:-1, 1:-1] - 2.0 * volt
        lap_x = padded[1:-1, 2:, 1:-1] + padded[1:-1, :-2, 1:-1] - 2.0 * volt
        lap_y = padded[1:-1, 1:-1, 2:] + padded[1:-1, 1:-1, :-2] - 2.0 * volt
        react_v, new_w = cell_kinetics(volt, recovery, into_voxel)
        new_v = volt + (coef_z * lap_z + coef_x * lap_x + coef_y * lap_y) + react_v
        cable = jnp.pad(term_volt, ((0, 0), (1, 1)), mode="edge")
        lap_k = cable[:, 2:] + cable[:, :-2] - 2.0 * term_volt
        react_u, new_r = cell_kinetics(term_volt, term_recovery, 0.1 * into_term)
        new_u = term_volt + cable_gain[:, None] * lap_k + react_u
        volt, recovery, term_volt, term_recovery = (new_v, new_w, new_u, new_r)
    return (volt, recovery, term_volt, term_recovery)


def solution(mesh):
    return jax.shard_map(
        on_device,
        mesh=mesh,
        in_specs=(
            P("gz", "gx", "gy"),
            P("gz", "gx", "gy"),
            P("gz", "gx", "gy"),
            P(),
            P(("gx", "gy", "gz")),
            P(("gx", "gy", "gz")),
            P(("gx", "gy", "gz"), None),
            P(("gx", "gy", "gz"), None),
            P(("gx", "gy", "gz"), None),
            P(("gx", "gy", "gz")),
            P(("gx", "gy", "gz")),
        ),
        out_specs=(
            P("gz", "gx", "gy"),
            P("gz", "gx", "gy"),
            P(("gx", "gy", "gz"), None),
            P(("gx", "gy", "gz"), None),
        ),
        check_vma=False,
    )
```

profile of v0, /device:TPU:0, one launch (start us, length us, event | category | flops | bytes accessed | tf_op | source)
XLA Modules:
  0.0 290.0 jit_solution(17605327394205154971)
XLA Ops:
  1.5 4.9 %collective-permute-start = (f32[16,1,128]{2,1,0:T(1,128)S(1)}, f32[16,1,128]{2,1,0:T(1,128)S(1)}, u32[]{:S(2)}, u32[]{:S(2)}) collective-permute-start(f32[16,1,128]{2,1,0:T(1,128)S(1)} %get-tuple-element.54), channel_id=1, source_target_pairs={{0,8},{8,16},{16,24},{1,9},{9,17},{17,25},{2,10},{10,18},{18,26},{... | collective-permute-start | bytes 24584 | tf_op jit(solution)/shard_map/ppermute | solution.py:18
  6.5 1.3 collective-permute-start.1
  9.8 8.1 %all-to-all-start = ((s32[16,16,1]{1,2,0:T(1,128)}), s32[16,16,1]{1,2,0:T(1,128)S(1)}, u32[]{:S(2)}, u32[]{:S(2)}) async-start(s32[16,16,1]{1,2,0:T(1,128)} %all_to_all.64), calls=%async_computation | async-start | bytes 16384 | tf_op jit(solution)/shard_map/all_to_all | solution.py:86
  21.4 2.0 broadcast_compare_fusion
  23.9 1.9 scatter_custom_fusion.1
  25.8 6.9 %all-to-all-start.1 = ((f32[16,16,128]{2,1,0:T(8,128)}), f32[16,16,128]{2,1,0:T(8,128)S(1)}, u32[]{:S(2)}, u32[]{:S(2)}) async-start(f32[16,16,128]{2,1,0:T(8,128)} %bitcast.64), calls=%async_computation.1 | async-start | bytes 262144 | tf_op jit(solution)/shard_map/all_to_all | solution.py:94
  34.8 3.8 %collective-permute-start.2 = (f32[16,34,1]{2,1,0:T(8,128)S(1)}, f32[16,34,1]{2,1,0:T(8,128)S(1)}, u32[]{:S(2)}, u32[]{:S(2)}) collective-permute-start(f32[16,34,1]{2,1,0:T(8,128)S(1)} %get-tuple-element.38), channel_id=1, source_target_pairs={{0,2},{2,4},{4,6},{1,3},{3,5},{5,7},{8,10},{10,12},{12,14},{9,11},... | collective-permute-start | bytes 6536 | tf_op jit(solution)/shard_map/ppermute | solution.py:18
  38.7 1.3 collective-permute-start.3
  40.0 20.5 %broadcast_select_fusion.16 = (f32[256]{0:T(256)}, f32[256]{0:T(256)S(1)}) fusion(pred[256]{0:T(512)(128)(4,1)S(1)} %ge.29, f32[]{:T(128)} %bitcast.61, f32[]{:T(128)} %bitcast.60, s32[256]{0:T(256)S(1)} %bitcast.132, f32[]{:T(128)} %bitcast.59, f32[]{:T(128)} %bitcast.58, f32[]{:T(128)} %bitcast.57, f32[]{:T(128)} %bitcast.56, f32[]{:T(128)} %bitcast.55, ...), kind=kLoop, calls=%fused_computation.329 | loop fusion | flops 16128 | bytes 3456 | tf_op jit(solution)/shard_map/jit(_where)/select_n | solution.py:89
  60.7 1.3 collective-permute-start.5
  62.9 1.3 collective-permute-start.4
  69.5 7.6 %all-to-all-start.2 = ((f32[16,16,128]{2,1,0:T(8,128)}), f32[16,16,128]{2,1,0:T(8,128)S(1)}, u32[]{:S(2)}, u32[]{:S(2)}) async-start(f32[16,16,128]{2,1,0:T(8,128)} %subtract_multiply_fusion.3), calls=%async_computation.2 | async-start | bytes 262144 | tf_op jit(solution)/shard_map/all_to_all | solution.py:96
  78.3 6.6 %all-to-all-done.2 = f32[16,16,128]{2,1,0:T(8,128)S(1)} async-done(((f32[16,16,128]{2,1,0:T(8,128)}), f32[16,16,128]{2,1,0:T(8,128)S(1)}, u32[]{:S(2)}, u32[]{:S(2)}) %all-to-all-start.2) | async-done | bytes 131104 | tf_op jit(solution)/shard_map/all_to_all | solution.py:96
  85.0 1.6 scatter_custom_fusion.2
  87.5 17.8 %fusion.41 = (f32[16,32,128]{2,1,0:T(8,128)S(1)}, f32[16,32,128]{2,1,0:T(8,128)S(1)}, f32[16,32,128]{2,1,0:T(8,128)S(1)}, f32[16,32,128]{2,1,0:T(8,128)}) fusion(f32[16,32,128]{2,1,0:T(8,128)S(1)} %copy-done.1, f32[18,34,128]{2,1,0:T(8,128)} %slice.646, f32[18,34,1]{2,1,0:T(8,128)} %get-tuple-element.31, f32[18,34,1]{2,1,0:T(8,128)} %get-tuple-element.30, ...), kind=kLoop, calls=%fused_computation.132 | loop fusion | flops 3997696 | bytes 3051968 | tf_op jit(solution)/shard_map/add | solution.py:109
  105.2 2.8 collective-permute-start.6
  108.0 1.3 collective-permute-start.7
  109.4 4.2 %collective-permute-done.7 = f32[16,1,128]{2,1,0:T(1,128)S(1)} collective-permute-done((f32[16,1,128]{2,1,0:T(1,128)S(1)}, f32[16,1,128]{2,1,0:T(1,128)S(1)}, u32[]{:S(2)}, u32[]{:S(2)}) %collective-permute-start.7) | collective-permute-done | bytes 8224 | tf_op jit(solution)/shard_map/ppermute | solution.py:20
  113.8 2.5 collective-permute-start.8
  116.3 1.3 collective-permute-start.9
  117.6 3.2 %collective-permute-done.8 = f32[16,34,1]{2,1,0:T(8,128)S(1)} collective-permute-done((f32[16,34,1]{2,1,0:T(8,128)S(1)}, f32[16,34,1]{2,1,0:T(8,128)S(1)}, u32[]{:S(2)}, u32[]{:S(2)}) %collective-permute-start.8) | collective-permute-done | bytes 2208 | tf_op jit(solution)/shard_map/ppermute | solution.py:18
  120.8 8.9 %collective-permute-done.9 = f32[16,34,1]{2,1,0:T(8,128)S(1)} collective-permute-done((f32[16,34,1]{2,1,0:T(8,128)S(1)}, f32[16,34,1]{2,1,0:T(8,128)S(1)}, u32[]{:S(2)}, u32[]{:S(2)}) %collective-permute-start.9) | collective-permute-done | bytes 2208 | tf_op jit(solution)/shard_map/ppermute | solution.py:20
  129.8 1.3 collective-permute-start.11
  131.2 1.7 scatter_custom_fusion.3
  133.0 1.3 collective-permute-start.10
  135.9 2.0 scatter_custom_fusion.4
  137.9 3.8 %all-to-all-start.3 = ((f32[16,16,128]{2,1,0:T(8,128)}), f32[16,16,128]{2,1,0:T(8,128)S(1)}, u32[]{:S(2)}, u32[]{:S(2)}) async-start(f32[16,16,128]{2,1,0:T(8,128)} %bitcast.71), calls=%async_computation.3 | async-start | bytes 262144 | tf_op jit(solution)/shard_map/all_to_all | solution.py:94
  144.5 5.6 %all-to-all-done.3 = f32[16,16,128]{2,1,0:T(8,128)S(1)} async-done(((f32[16,16,128]{2,1,0:T(8,128)}), f32[16,16,128]{2,1,0:T(8,128)S(1)}, u32[]{:S(2)}, u32[]{:S(2)}) %all-to-all-start.3) | async-done | bytes 131104 | tf_op jit(solution)/shard_map/all_to_all | solution.py:94
  150.9 3.7 %all-to-all-start.4 = ((f32[16,16,128]{2,1,0:T(8,128)}), f32[16,16,128]{2,1,0:T(8,128)S(1)}, u32[]{:S(2)}, u32[]{:S(2)}) async-start(f32[16,16,128]{2,1,0:T(8,128)} %subtract_multiply_fusion.2), calls=%async_computation.4 | async-start | bytes 262144 | tf_op jit(solution)/shard_map/all_to_all | solution.py:96
  155.8 6.5 %all-to-all-done.4 = f32[16,16,128]{2,1,0:T(8,128)S(1)} async-done(((f32[16,16,128]{2,1,0:T(8,128)}), f32[16,16,128]{2,1,0:T(8,128)S(1)}, u32[]{:S(2)}, u32[]{:S(2)}) %all-to-all-start.4) | async-done | bytes 131104 | tf_op jit(solution)/shard_map/all_to_all | solution.py:96
  162.2 1.8 scatter_custom_fusion.5
  164.0 2.1 fusion.29
  166.1 2.8 collective-permute-start.12
  168.9 1.3 collective-permute-start.13
  170.3 4.2 %collective-permute-done.13 = f32[16,1,128]{2,1,0:T(1,128)S(1)} collective-permute-done((f32[16,1,128]{2,1,0:T(1,128)S(1)}, f32[16,1,128]{2,1,0:T(1,128)S(1)}, u32[]{:S(2)}, u32[]{:S(2)}) %collective-permute-start.13) | collective-permute-done | bytes 8224 | tf_op jit(solution)/shard_map/ppermute | solution.py:20
  174.7 2.5 collective-permute-start.14
  177.2 1.3 collective-permute-start.15
  178.5 3.2 %collective-permute-done.14 = f32[16,34,1]{2,1,0:T(8,128)S(1)} collective-permute-done((f32[16,34,1]{2,1,0:T(8,128)S(1)}, f32[16,34,1]{2,1,0:T(8,128)S(1)}, u32[]{:S(2)}, u32[]{:S(2)}) %collective-permute-start.14) | collective-permute-done | bytes 2208 | tf_op jit(solution)/shard_map/ppermute | solution.py:18
  181.7 8.8 %collective-permute-done.15 = f32[16,34,1]{2,1,0:T(8,128)S(1)} collective-permute-done((f32[16,34,1]{2,1,0:T(8,128)S(1)}, f32[16,34,1]{2,1,0:T(8,128)S(1)}, u32[]{:S(2)}, u32[]{:S(2)}) %collective-permute-start.15) | collective-permute-done | bytes 2208 | tf_op jit(solution)/shard_map/ppermute | solution.py:20
  190.7 1.3 collective-permute-start.17
  192.1 1.7 scatter_custom_fusion.6
  193.9 1.3 collective-permute-start.16
  196.8 2.0 scatter_custom_fusion.7
  198.8 3.8 %all-to-all-start.5 = ((f32[16,16,128]{2,1,0:T(8,128)}), f32[16,16,128]{2,1,0:T(8,128)S(1)}, u32[]{:S(2)}, u32[]{:S(2)}) async-start(f32[16,16,128]{2,1,0:T(8,128)} %bitcast.77), calls=%async_computation.5 | async-start | bytes 262144 | tf_op jit(solution)/shard_map/all_to_all | solution.py:94
  205.8 5.3 %all-to-all-done.5 = f32[16,16,128]{2,1,0:T(8,128)S(1)} async-done(((f32[16,16,128]{2,1,0:T(8,128)}), f32[16,16,128]{2,1,0:T(8,128)S(1)}, u32[]{:S(2)}, u32[]{:S(2)}) %all-to-all-start.5) | async-done | bytes 131104 | tf_op jit(solution)/shard_map/all_to_all | solution.py:94
  211.8 3.5 %all-to-all-start.6 = ((f32[16,16,128]{2,1,0:T(8,128)}), f32[16,16,128]{2,1,0:T(8,128)S(1)}, u32[]{:S(2)}, u32[]{:S(2)}) async-start(f32[16,16,128]{2,1,0:T(8,128)} %subtract_multiply_fusion.1), calls=%async_computation.6 | async-start | bytes 262144 | tf_op jit(solution)/shard_map/all_to_all | solution.py:96
  216.5 6.6 %all-to-all-done.6 = f32[16,16,128]{2,1,0:T(8,128)S(1)} async-done(((f32[16,16,128]{2,1,0:T(8,128)}), f32[16,16,128]{2,1,0:T(8,128)S(1)}, u32[]{:S(2)}, u32[]{:S(2)}) %all-to-all-start.6) | async-done | bytes 131104 | tf_op jit(solution)/shard_map/all_to_all | solution.py:96
  223.1 1.8 scatter_custom_fusion.8
  224.9 3.1 %multiply_add_fusion = (f32[16,32,128]{2,1,0:T(8,128)}, f32[16,32,128]{2,1,0:T(8,128)S(1)}, f32[16,32,128]{2,1,0:T(8,128)}) fusion(f32[16,32,128]{2,1,0:T(8,128)S(1)} %fusion.29, f32[16,32,128]{2,1,0:T(8,128)S(1)} %bitcast.124, f32[16,32,128]{2,1,0:T(8,128)} %get-tuple-element.21, f32[18,34,128]{2,1,0:T(8,128)} %slice.666, ...), kind=kLoop, calls=%fused_computation.153 | loop fusion | flops 4259840 | bytes 3576160 | tf_op jit(solution)/shard_map/add | solution.py:30
  228.0 2.8 collective-permute-start.18
  232.2 4.2 %collective-permute-done.19 = f32[16,1,128]{2,1,0:T(1,128)S(1)} collective-permute-done((f32[16,1,128]{2,1,0:T(1,128)S(1)}, f32[16,1,128]{2,1,0:T(1,128)S(1)}, u32[]{:S(2)}, u32[]{:S(2)}) %collective-permute-start.19) | collective-permute-done | bytes 8224 | tf_op jit(solution)/shard_map/ppermute | solution.py:20
  236.6 2.5 collective-permute-start.20
  240.5 1.7 scatter_custom_fusion.9
  242.2 1.4 collective-permute-done.20
  243.6 8.8 %collective-permute-done.21 = f32[16,34,1]{2,1,0:T(8,128)S(1)} collective-permute-done((f32[16,34,1]{2,1,0:T(8,128)S(1)}, f32[16,34,1]{2,1,0:T(8,128)S(1)}, u32[]{:S(2)}, u32[]{:S(2)}) %collective-permute-start.21) | collective-permute-done | bytes 2208 | tf_op jit(solution)/shard_map/ppermute | solution.py:20
  252.6 1.3 collective-permute-start.23
  257.6 2.0 scatter_custom_fusion.10
  259.6 3.7 %all-to-all-start.7 = ((f32[16,16,128]{2,1,0:T(8,128)}), f32[16,16,128]{2,1,0:T(8,128)S(1)}, u32[]{:S(2)}, u32[]{:S(2)}) async-start(f32[16,16,128]{2,1,0:T(8,128)} %bitcast.83), calls=%async_computation.7 | async-start | bytes 262144 | tf_op jit(solution)/shard_map/all_to_all | solution.py:94
  265.7 5.7 %all-to-all-done.7 = f32[16,16,128]{2,1,0:T(8,128)S(1)} async-done(((f32[16,16,128]{2,1,0:T(8,128)}), f32[16,16,128]{2,1,0:T(8,128)S(1)}, u32[]{:S(2)}, u32[]{:S(2)}) %all-to-all-start.7) | async-done | bytes 131104 | tf_op jit(solution)/shard_map/all_to_all | solution.py:94
  272.2 4.2 %all-to-all-start.8 = ((f32[16,16,128]{2,1,0:T(8,128)}), f32[16,16,128]{2,1,0:T(8,128)}, u32[]{:S(2)}, u32[]{:S(2)}) async-start(f32[16,16,128]{2,1,0:T(8,128)} %subtract_multiply_fusion), calls=%async_computation.8 | async-start | bytes 262144 | tf_op jit(solution)/shard_map/all_to_all | solution.py:96
  277.1 2.0 scatter_custom_fusion.12
  279.8 4.6 %all-to-all-done.8 = f32[16,16,128]{2,1,0:T(8,128)} async-done(((f32[16,16,128]{2,1,0:T(8,128)}), f32[16,16,128]{2,1,0:T(8,128)}, u32[]{:S(2)}, u32[]{:S(2)}) %all-to-all-start.8) | async-done | bytes 131104 | tf_op jit(solution)/shard_map/all_to_all | solution.py:96
  284.4 3.0 %scatter_custom_fusion.11 = f32[512,128]{1,0:T(8,128)} fusion(s32[128]{0:T(128)} %param.15, f32[]{:T(128)} %constant.37.clone.1, f32[256,128]{1,0:T(8,128)} %bitcast.84, s32[1024]{0:T(1024)} %copy-done.43), kind=kCustom, calls=%fused_computation.176 | custom fusion | flops 16384 | bytes 262656 | tf_op jit(solution)/shard_map/scatter-add | solution.py:97
  287.4 2.6 fusion.5
  (208 shorter events, 42.5 us)
Async XLA Ops:
  1.5 33.1 %collective-permute-start = (f32[16,1,128]{2,1,0:T(1,128)S(1)}, f32[16,1,128]{2,1,0:T(1,128)S(1)}, u32[]{:S(2)}, u32[]{:S(2)}) collective-permute-start(f32[16,1,128]{2,1,0:T(1,128)S(1)} %get-tuple-element.54), channel_id=1, source_target_pairs={{0,8},{8,16},{16,24},{1,9},{9,17},{17,25},{2,10},{10,18},{18,26},{... | collective-permute-start | bytes 24584 | tf_op jit(solution)/shard_map/ppermute | solution.py:18
  6.5 1.3 copy-start.46
  6.5 28.2 %collective-permute-start.1 = (f32[16,1,128]{2,1,0:T(1,128)S(1)}, f32[16,1,128]{2,1,0:T(1,128)S(1)}, u32[]{:S(2)}, u32[]{:S(2)}) collective-permute-start(f32[16,1,128]{2,1,0:T(1,128)S(1)} %get-tuple-element.55), channel_id=1, source_target_pairs={{8,0},{16,8},{24,16},{9,1},{17,9},{25,17},{10,2},{18,10},{26,18},{... | collective-permute-start | bytes 24584 | tf_op jit(solution)/shard_map/ppermute | solution.py:20
  8.0 15.4 %copy-start.45 = (s32[128]{0:T(128)}, s32[128]{0:T(128)S(1)}, u32[]{:S(2)}) copy-start(s32[128]{0:T(128)S(1)} %fusion.109) | copy-start | bytes 1540
  9.8 8.1 %copy-start.13 = (f32[32]{0:T(128)S(1)}, f32[32]{0:T(128)}, u32[]{:S(2)}) copy-start(f32[32]{0:T(128)} %param.20) | copy-start | bytes 388
  9.8 16.0 %all-to-all-start = ((s32[16,16,1]{1,2,0:T(1,128)}), s32[16,16,1]{1,2,0:T(1,128)S(1)}, u32[]{:S(2)}, u32[]{:S(2)}) async-start(s32[16,16,1]{1,2,0:T(1,128)} %all_to_all.64), calls=%async_computation | async-start | bytes 16384 | tf_op jit(solution)/shard_map/all_to_all | solution.py:86
  20.0 65.0 %copy-start.43 = (s32[1024]{0:T(1024)}, s32[1024]{0:T(1024)S(1)}, u32[]{:S(2)}) copy-start(s32[1024]{0:T(1024)S(1)} %pad_clamp_fusion) | copy-start | bytes 12292
  21.4 2.6 copy-start.1
  25.8 43.0 %all-to-all-start.1 = ((f32[16,16,128]{2,1,0:T(8,128)}), f32[16,16,128]{2,1,0:T(8,128)S(1)}, u32[]{:S(2)}, u32[]{:S(2)}) async-start(f32[16,16,128]{2,1,0:T(8,128)} %bitcast.64), calls=%async_computation.1 | async-start | bytes 262144 | tf_op jit(solution)/shard_map/all_to_all | solution.py:94
  34.8 25.7 %collective-permute-start.2 = (f32[16,34,1]{2,1,0:T(8,128)S(1)}, f32[16,34,1]{2,1,0:T(8,128)S(1)}, u32[]{:S(2)}, u32[]{:S(2)}) collective-permute-start(f32[16,34,1]{2,1,0:T(8,128)S(1)} %get-tuple-element.38), channel_id=1, source_target_pairs={{0,2},{2,4},{4,6},{1,3},{3,5},{5,7},{8,10},{10,12},{12,14},{9,11},... | collective-permute-start | bytes 6536 | tf_op jit(solution)/shard_map/ppermute | solution.py:18
  38.7 21.9 %collective-permute-start.3 = (f32[16,34,1]{2,1,0:T(8,128)S(1)}, f32[16,34,1]{2,1,0:T(8,128)S(1)}, u32[]{:S(2)}, u32[]{:S(2)}) collective-permute-start(f32[16,34,1]{2,1,0:T(8,128)S(1)} %get-tuple-element.39), channel_id=1, source_target_pairs={{2,0},{4,2},{6,4},{3,1},{5,3},{7,5},{10,8},{12,10},{14,12},{11,9},... | collective-permute-start | bytes 6536 | tf_op jit(solution)/shard_map/ppermute | solution.py:20
  60.7 2.2 collective-permute-start.5
  62.0 6.8 %copy-start.20 = (f32[16,16]{1,0:T(8,128)}, f32[16,16]{1,0:T(8,128)S(1)}, u32[]{:S(2)}) copy-start(f32[16,16]{1,0:T(8,128)S(1)} %bitcast_select_fusion) | copy-start | bytes 3076
  62.8 1.4 copy-start
  62.9 3.1 %collective-permute-start.4 = (f32[1,34,130]{2,1,0:T(8,128)S(1)}, f32[1,34,130]{2,1,0:T(8,128)S(1)}, u32[]{:S(2)}, u32[]{:S(2)}) collective-permute-start(f32[1,34,130]{2,1,0:T(8,128)S(1)} %get-tuple-element.23), channel_id=1, source_target_pairs={{1,0},{3,2},{5,4},{7,6},{9,8},{11,10},{13,12},{15,14},{17,16},{19,... | collective-permute-start | bytes 53048 | tf_op jit(solution)/shard_map/ppermute | solution.py:20
  65.0 3.8 %copy-start.7 = (f32[256,128]{1,0:T(8,128)}, f32[256,128]{1,0:T(8,128)S(1)}, u32[]{:S(2)}) copy-start(f32[256,128]{1,0:T(8,128)S(1)} %gather_fusion) | copy-start | bytes 393220
  69.5 15.4 %all-to-all-start.2 = ((f32[16,16,128]{2,1,0:T(8,128)}), f32[16,16,128]{2,1,0:T(8,128)S(1)}, u32[]{:S(2)}, u32[]{:S(2)}) async-start(f32[16,16,128]{2,1,0:T(8,128)} %subtract_multiply_fusion.3), calls=%async_computation.2 | async-start | bytes 262144 | tf_op jit(solution)/shard_map/all_to_all | solution.py:96
  78.3 8.3 %copy-start.6 = (f32[16,32,128]{2,1,0:T(8,128)S(1)}, f32[16,32,128]{2,1,0:T(8,128)}, u32[]{:S(2)}) copy-start(f32[16,32,128]{2,1,0:T(8,128)} %param.12) | copy-start | bytes 786436
  105.2 58.8 %copy-start.2 = (f32[16,32,128]{2,1,0:T(8,128)}, f32[16,32,128]{2,1,0:T(8,128)S(1)}, u32[]{:S(2)}) copy-start(f32[16,32,128]{2,1,0:T(8,128)S(1)} %get-tuple-element.20) | copy-start | bytes 786436
  105.2 4.1 %collective-permute-start.6 = (f32[16,1,128]{2,1,0:T(1,128)S(1)}, f32[16,1,128]{2,1,0:T(1,128)S(1)}, u32[]{:S(2)}, u32[]{:S(2)}) collective-permute-start(f32[16,1,128]{2,1,0:T(1,128)S(1)} %get-tuple-element.44), channel_id=1, source_target_pairs={{0,8},{8,16},{16,24},{1,9},{9,17},{17,25},{2,10},{10,18},{18,26},{... | collective-permute-start | bytes 24584 | tf_op jit(solution)/shard_map/ppermute | solution.py:18
  108.0 5.5 %collective-permute-start.7 = (f32[16,1,128]{2,1,0:T(1,128)S(1)}, f32[16,1,128]{2,1,0:T(1,128)S(1)}, u32[]{:S(2)}, u32[]{:S(2)}) collective-permute-start(f32[16,1,128]{2,1,0:T(1,128)S(1)} %get-tuple-element.45), channel_id=1, source_target_pairs={{8,0},{16,8},{24,16},{9,1},{17,9},{25,17},{10,2},{18,10},{26,18},{... | collective-permute-start | bytes 24584 | tf_op jit(solution)/shard_map/ppermute | solution.py:20
  113.8 7.1 %collective-permute-start.8 = (f32[16,34,1]{2,1,0:T(8,128)S(1)}, f32[16,34,1]{2,1,0:T(8,128)S(1)}, u32[]{:S(2)}, u32[]{:S(2)}) collective-permute-start(f32[16,34,1]{2,1,0:T(8,128)S(1)} %get-tuple-element.36), channel_id=1, source_target_pairs={{0,2},{2,4},{4,6},{1,3},{3,5},{5,7},{8,10},{10,12},{12,14},{9,11},... | collective-permute-start | bytes 6536 | tf_op jit(solution)/shard_map/ppermute | solution.py:18
  116.3 13.4 %collective-permute-start.9 = (f32[16,34,1]{2,1,0:T(8,128)S(1)}, f32[16,34,1]{2,1,0:T(8,128)S(1)}, u32[]{:S(2)}, u32[]{:S(2)}) collective-permute-start(f32[16,34,1]{2,1,0:T(8,128)S(1)} %get-tuple-element.37), channel_id=1, source_target_pairs={{2,0},{4,2},{6,4},{3,1},{5,3},{7,5},{10,8},{12,10},{14,12},{11,9},... | collective-permute-start | bytes 6536 | tf_op jit(solution)/shard_map/ppermute | solution.py:20
  117.6 13.4 %copy-start.8 = (f32[256,128]{1,0:T(8,128)S(1)}, f32[256,128]{1,0:T(8,128)}, u32[]{:S(2)}) copy-start(f32[256,128]{1,0:T(8,128)} %copy-done.7) | copy-start | bytes 393220
  129.8 1.3 copy-start.36
  129.8 3.1 %collective-permute-start.11 = (f32[1,34,130]{2,1,0:T(8,128)S(1)}, f32[1,34,130]{2,1,0:T(8,128)S(1)}, u32[]{:S(2)}, u32[]{:S(2)}) collective-permute-start(f32[1,34,130]{2,1,0:T(8,128)S(1)} %pad_maximum_fusion.82), channel_id=1, source_target_pairs={{0,1},{2,3},{4,5},{6,7},{8,9},{10,11},{12,13},{14,15},{16,17},{18,... | collective-permute-start | bytes 53048 | tf_op jit(solution)/shard_map/ppermute | solution.py:18
  132.9 1.4 copy-start.32
  133.0 8.8 %collective-permute-start.10 = (f32[1,34,130]{2,1,0:T(8,128)S(1)}, f32[1,34,130]{2,1,0:T(8,128)S(1)}, u32[]{:S(2)}, u32[]{:S(2)}) collective-permute-start(f32[1,34,130]{2,1,0:T(8,128)S(1)} %get-tuple-element.17), channel_id=1, source_target_pairs={{1,0},{3,2},{5,4},{7,6},{9,8},{11,10},{13,12},{15,14},{17,16},{19,... | collective-permute-start | bytes 53048 | tf_op jit(solution)/shard_map/ppermute | solution.py:20
  135.9 14.2 %copy-start.9 = (f32[256,128]{1,0:T(8,128)}, f32[256,128]{1,0:T(8,128)S(1)}, u32[]{:S(2)}) copy-start(f32[256,128]{1,0:T(8,128)S(1)} %gather_fusion.1) | copy-start | bytes 393220
  137.9 12.2 %all-to-all-start.3 = ((f32[16,16,128]{2,1,0:T(8,128)}), f32[16,16,128]{2,1,0:T(8,128)S(1)}, u32[]{:S(2)}, u32[]{:S(2)}) async-start(f32[16,16,128]{2,1,0:T(8,128)} %bitcast.71), calls=%async_computation.3 | async-start | bytes 262144 | tf_op jit(solution)/shard_map/all_to_all | solution.py:94
  143.6 6.5 %copy-start.21 = (f32[16,16]{1,0:T(8,128)S(1)}, f32[16,16]{1,0:T(8,128)}, u32[]{:S(2)}) copy-start(f32[16,16]{1,0:T(8,128)} %copy-done.20) | copy-start | bytes 3076
  150.9 11.3 %all-to-all-start.4 = ((f32[16,16,128]{2,1,0:T(8,128)}), f32[16,16,128]{2,1,0:T(8,128)S(1)}, u32[]{:S(2)}, u32[]{:S(2)}) async-start(f32[16,16,128]{2,1,0:T(8,128)} %subtract_multiply_fusion.2), calls=%async_computation.4 | async-start | bytes 262144 | tf_op jit(solution)/shard_map/all_to_all | solution.py:96
  155.8 8.3 %copy-start.4 = (f32[16,32,128]{2,1,0:T(8,128)S(1)}, f32[16,32,128]{2,1,0:T(8,128)}, u32[]{:S(2)}) copy-start(f32[16,32,128]{2,1,0:T(8,128)} %get-tuple-element.21) | copy-start | bytes 786436
  166.1 4.2 %collective-permute-start.12 = (f32[16,1,128]{2,1,0:T(1,128)S(1)}, f32[16,1,128]{2,1,0:T(1,128)S(1)}, u32[]{:S(2)}, u32[]{:S(2)}) collective-permute-start(f32[16,1,128]{2,1,0:T(1,128)S(1)} %get-tuple-element.42), channel_id=1, source_target_pairs={{0,8},{8,16},{16,24},{1,9},{9,17},{17,25},{2,10},{10,18},{18,26},{... | collective-permute-start | bytes 24584 | tf_op jit(solution)/shard_map/ppermute | solution.py:18
  168.9 5.5 %collective-permute-start.13 = (f32[16,1,128]{2,1,0:T(1,128)S(1)}, f32[16,1,128]{2,1,0:T(1,128)S(1)}, u32[]{:S(2)}, u32[]{:S(2)}) collective-permute-start(f32[16,1,128]{2,1,0:T(1,128)S(1)} %get-tuple-element.43), channel_id=1, source_target_pairs={{8,0},{16,8},{24,16},{9,1},{17,9},{25,17},{10,2},{18,10},{26,18},{... | collective-permute-start | bytes 24584 | tf_op jit(solution)/shard_map/ppermute | solution.py:20
  170.3 32.8 %copy-start.14 = (f32[16,1,128]{2,1,0:T(1,128)}, f32[16,1,128]{2,1,0:T(1,128)S(1)}, u32[]{:S(2)}) copy-start(f32[16,1,128]{2,1,0:T(1,128)S(1)} %collective-permute-done.12) | copy-start | bytes 24580
  174.5 28.6 %copy-start.17 = (f32[16,1,128]{2,1,0:T(1,128)}, f32[16,1,128]{2,1,0:T(1,128)S(1)}, u32[]{:S(2)}) copy-start(f32[16,1,128]{2,1,0:T(1,128)S(1)} %collective-permute-done.13) | copy-start | bytes 24580
  174.7 7.0 %collective-permute-start.14 = (f32[16,34,1]{2,1,0:T(8,128)S(1)}, f32[16,34,1]{2,1,0:T(8,128)S(1)}, u32[]{:S(2)}, u32[]{:S(2)}) collective-permute-start(f32[16,34,1]{2,1,0:T(8,128)S(1)} %get-tuple-element.34), channel_id=1, source_target_pairs={{0,2},{2,4},{4,6},{1,3},{3,5},{5,7},{8,10},{10,12},{12,14},{9,11},... | collective-permute-start | bytes 6536 | tf_op jit(solution)/shard_map/ppermute | solution.py:18
  177.2 13.4 %collective-permute-start.15 = (f32[16,34,1]{2,1,0:T(8,128)S(1)}, f32[16,34,1]{2,1,0:T(8,128)S(1)}, u32[]{:S(2)}, u32[]{:S(2)}) collective-permute-start(f32[16,34,1]{2,1,0:T(8,128)S(1)} %get-tuple-element.35), channel_id=1, source_target_pairs={{2,0},{4,2},{6,4},{3,1},{5,3},{7,5},{10,8},{12,10},{14,12},{11,9},... | collective-permute-start | bytes 6536 | tf_op jit(solution)/shard_map/ppermute | solution.py:20
  178.5 13.4 %copy-start.10 = (f32[256,128]{1,0:T(8,128)S(1)}, f32[256,128]{1,0:T(8,128)}, u32[]{:S(2)}) copy-start(f32[256,128]{1,0:T(8,128)} %copy-done.9) | copy-start | bytes 393220
  178.5 13.4 %copy-start.37 = (f32[256]{0:T(256)S(1)}, f32[256]{0:T(256)}, u32[]{:S(2)}) copy-start(f32[256]{0:T(256)} %get-tuple-element.14) | copy-start | bytes 3076
  190.7 3.1 %collective-permute-start.17 = (f32[1,34,130]{2,1,0:T(8,128)S(1)}, f32[1,34,130]{2,1,0:T(8,128)S(1)}, u32[]{:S(2)}, u32[]{:S(2)}) collective-permute-start(f32[1,34,130]{2,1,0:T(8,128)S(1)} %pad_maximum_fusion.77), channel_id=1, source_target_pairs={{0,1},{2,3},{4,5},{6,7},{8,9},{10,11},{12,13},{14,15},{16,17},{18,... | collective-permute-start | bytes 53048 | tf_op jit(solution)/shard_map/ppermute | solution.py:18
  193.8 1.4 copy-start.33
  193.9 8.7 %collective-permute-start.16 = (f32[1,34,130]{2,1,0:T(8,128)S(1)}, f32[1,34,130]{2,1,0:T(8,128)S(1)}, u32[]{:S(2)}, u32[]{:S(2)}) collective-permute-start(f32[1,34,130]{2,1,0:T(8,128)S(1)} %get-tuple-element.13), channel_id=1, source_target_pairs={{1,0},{3,2},{5,4},{7,6},{9,8},{11,10},{13,12},{15,14},{17,16},{19,... | collective-permute-start | bytes 53048 | tf_op jit(solution)/shard_map/ppermute | solution.py:20
  196.8 14.2 %copy-start.11 = (f32[256,128]{1,0:T(8,128)}, f32[256,128]{1,0:T(8,128)S(1)}, u32[]{:S(2)}) copy-start(f32[256,128]{1,0:T(8,128)S(1)} %gather_fusion.2) | copy-start | bytes 393220
  198.8 12.2 %all-to-all-start.5 = ((f32[16,16,128]{2,1,0:T(8,128)}), f32[16,16,128]{2,1,0:T(8,128)S(1)}, u32[]{:S(2)}, u32[]{:S(2)}) async-start(f32[16,16,128]{2,1,0:T(8,128)} %bitcast.77), calls=%async_computation.5 | async-start | bytes 262144 | tf_op jit(solution)/shard_map/all_to_all | solution.py:94
  203.3 0.9 copy-start.28
  204.8 6.2 %copy-start.22 = (f32[16,16]{1,0:T(8,128)S(1)}, f32[16,16]{1,0:T(8,128)}, u32[]{:S(2)}) copy-start(f32[16,16]{1,0:T(8,128)} %copy-done.20) | copy-start | bytes 3076
  211.8 11.3 %all-to-all-start.6 = ((f32[16,16,128]{2,1,0:T(8,128)}), f32[16,16,128]{2,1,0:T(8,128)S(1)}, u32[]{:S(2)}, u32[]{:S(2)}) async-start(f32[16,16,128]{2,1,0:T(8,128)} %subtract_multiply_fusion.1), calls=%async_computation.6 | async-start | bytes 262144 | tf_op jit(solution)/shard_map/all_to_all | solution.py:96
  216.5 8.4 %copy-start.3 = (f32[16,32,128]{2,1,0:T(8,128)S(1)}, f32[16,32,128]{2,1,0:T(8,128)}, u32[]{:S(2)}) copy-start(f32[16,32,128]{2,1,0:T(8,128)} %copy-done.2) | copy-start | bytes 786436
  223.1 1.8 copy-start.16
  228.0 4.2 %collective-permute-start.18 = (f32[16,1,128]{2,1,0:T(1,128)S(1)}, f32[16,1,128]{2,1,0:T(1,128)S(1)}, u32[]{:S(2)}, u32[]{:S(2)}) collective-permute-start(f32[16,1,128]{2,1,0:T(1,128)S(1)} %get-tuple-element.40), channel_id=1, source_target_pairs={{0,8},{8,16},{16,24},{1,9},{9,17},{17,25},{2,10},{10,18},{18,26},{... | collective-permute-start | bytes 24584 | tf_op jit(solution)/shard_map/ppermute | solution.py:18
  230.8 5.5 %collective-permute-start.19 = (f32[16,1,128]{2,1,0:T(1,128)S(1)}, f32[16,1,128]{2,1,0:T(1,128)S(1)}, u32[]{:S(2)}, u32[]{:S(2)}) collective-permute-start(f32[16,1,128]{2,1,0:T(1,128)S(1)} %get-tuple-element.41), channel_id=1, source_target_pairs={{8,0},{16,8},{24,16},{9,1},{17,9},{25,17},{10,2},{18,10},{26,18},{... | collective-permute-start | bytes 24584 | tf_op jit(solution)/shard_map/ppermute | solution.py:20
  236.4 4.0 %copy-start.12 = (f32[256,128]{1,0:T(8,128)S(1)}, f32[256,128]{1,0:T(8,128)}, u32[]{:S(2)}) copy-start(f32[256,128]{1,0:T(8,128)} %copy-done.11) | copy-start | bytes 393220
  236.6 3.8 %copy-start.38 = (f32[256]{0:T(256)S(1)}, f32[256]{0:T(256)}, u32[]{:S(2)}) copy-start(f32[256]{0:T(256)} %get-tuple-element.14) | copy-start | bytes 3076
  236.6 7.0 %collective-permute-start.20 = (f32[16,34,1]{2,1,0:T(8,128)S(1)}, f32[16,34,1]{2,1,0:T(8,128)S(1)}, u32[]{:S(2)}, u32[]{:S(2)}) collective-permute-start(f32[16,34,1]{2,1,0:T(8,128)S(1)} %get-tuple-element.32), channel_id=1, source_target_pairs={{0,2},{2,4},{4,6},{1,3},{3,5},{5,7},{8,10},{10,12},{12,14},{9,11},... | collective-permute-start | bytes 6536 | tf_op jit(solution)/shard_map/ppermute | solution.py:18
  239.1 13.4 %collective-permute-start.21 = (f32[16,34,1]{2,1,0:T(8,128)S(1)}, f32[16,34,1]{2,1,0:T(8,128)S(1)}, u32[]{:S(2)}, u32[]{:S(2)}) collective-permute-start(f32[16,34,1]{2,1,0:T(8,128)S(1)} %get-tuple-element.33), channel_id=1, source_target_pairs={{2,0},{4,2},{6,4},{3,1},{5,3},{7,5},{10,8},{12,10},{14,12},{11,9},... | collective-permute-start | bytes 6536 | tf_op jit(solution)/shard_map/ppermute | solution.py:20
  242.2 11.7 %copy-start.34 = (f32[32,128]{1,0:T(8,128)S(1)}, f32[32,128]{1,0:T(8,128)}, u32[]{:S(2)}) copy-start(f32[32,128]{1,0:T(8,128)} %param.19) | copy-start | bytes 49156
  252.6 2.7 collective-permute-start.23
  255.3 8.0 %collective-permute-start.22 = (f32[1,34,130]{2,1,0:T(8,128)S(1)}, f32[1,34,130]{2,1,0:T(8,128)S(1)}, u32[]{:S(2)}, u32[]{:S(2)}) collective-permute-start(f32[1,34,130]{2,1,0:T(8,128)S(1)} %get-tuple-element.11), channel_id=1, source_target_pairs={{1,0},{3,2},{5,4},{7,6},{9,8},{11,10},{13,12},{15,14},{17,16},{19,... | collective-permute-start | bytes 53048 | tf_op jit(solution)/shard_map/ppermute | solution.py:20
  259.6 11.8 %all-to-all-start.7 = ((f32[16,16,128]{2,1,0:T(8,128)}), f32[16,16,128]{2,1,0:T(8,128)S(1)}, u32[]{:S(2)}, u32[]{:S(2)}) async-start(f32[16,16,128]{2,1,0:T(8,128)} %bitcast.83), calls=%async_computation.7 | async-start | bytes 262144 | tf_op jit(solution)/shard_map/all_to_all | solution.py:94
  264.5 6.9 %copy-start.23 = (f32[16,16]{1,0:T(8,128)S(1)}, f32[16,16]{1,0:T(8,128)}, u32[]{:S(2)}) copy-start(f32[16,16]{1,0:T(8,128)} %copy-done.20) | copy-start | bytes 3076
  272.2 12.2 %all-to-all-start.8 = ((f32[16,16,128]{2,1,0:T(8,128)}), f32[16,16,128]{2,1,0:T(8,128)}, u32[]{:S(2)}, u32[]{:S(2)}) async-start(f32[16,16,128]{2,1,0:T(8,128)} %subtract_multiply_fusion), calls=%async_computation.8 | async-start | bytes 262144 | tf_op jit(solution)/shard_map/all_to_all | solution.py:96
  277.1 10.3 %copy-start.5 = (f32[16,32,128]{2,1,0:T(8,128)S(1)}, f32[16,32,128]{2,1,0:T(8,128)}, u32[]{:S(2)}) copy-start(f32[16,32,128]{2,1,0:T(8,128)} %get-tuple-element.21) | copy-start | bytes 786436
  (17 other events, 11.6 us)
where the time goes:
time: 293 us; the launch traced here: 290 us
  starting transfers between devices  90.7 us (31%)
  waiting for transfers between devices  89.9 us (31%)
  other arithmetic  79.3 us (27%)
  local copies, waits for them, and re-layouts  28.3 us (10%)
    ppermute x12, waiting for transfers between devices, extended(): lax.ppermute(head, axis, [((i + 1) % count, i) for i in range(ends)])  40.2 us
    ppermute x12, starting transfers between devices, extended(): lax.ppermute(tail, axis, [(i, (i + 1) % count) for i in range(ends)])  29.8 us
    all_to_all x4, waiting for transfers between devices, on_device(): lax.all_to_all(current, ('gx', 'gy'), split_axis=0, concat_axis=0, tiled=...  24.4 us
    add x3, other arithmetic, on_device(): new_v = volt + (coef_z * lap_z + coef_x * lap_x + coef_y * lap_y) + react_v  22.4 us
    select_n x2, other arithmetic, on_device(): gains = jnp.where(valid, term_gain[safe_ids], 0.0)  20.5 us
    all_to_all x4, starting transfers between devices, on_device(): lax.all_to_all(current, ('gx', 'gy'), split_axis=0, concat_axis=0, tiled=...  19 us
    all_to_all x4, starting transfers between devices, on_device(): lax.all_to_all(sent, ('gx', 'gy'), split_axis=0, concat_axis=0, tiled=True)  18.3 us
    all_to_all x4, waiting for transfers between devices, on_device(): lax.all_to_all(sent, ('gx', 'gy'), split_axis=0, concat_axis=0, tiled=True)  16.6 us
  transfers between devices with their start and end apart: 33, of which 18 were waited for; matrix products, arithmetic and copies ran while one was open for 21% of the time, Pallas kernels for 0%

commit v1 on v0

v1 whole, which is shorter than its diff:
```python
import functools
import jax
import jax.numpy as jnp
from jax import lax
from jax.experimental import pallas as pl
from jax.experimental.pallas import tpu as pltpu
from jax.sharding import PartitionSpec as P

STEPS = 4
MESH = pl.DeviceIdType.MESH
F32 = jnp.float32
BF16 = jnp.bfloat16
EXACT = lax.Precision.HIGHEST
GAIN_LANE = 64


def iota(shape, dim):
    return lax.broadcasted_iota(jnp.int32, shape, dim)


def one_hot(cond):
    return jnp.where(cond, 1.0, 0.0).astype(BF16)


def dot_nt(a, b):
    return lax.dot_general(a, b, (((1,), (1,)), ((), ())), preferred_element_type=F32)


def select_dot(mask, values):
    high = values.astype(BF16)
    rest = values - high.astype(F32)
    mid = rest.astype(BF16)
    low = (rest - mid.astype(F32)).astype(BF16)
    return (
        jnp.dot(mask, low, preferred_element_type=F32)
        + jnp.dot(mask, mid, preferred_element_type=F32)
    ) + jnp.dot(mask, high, preferred_element_type=F32)


def kernel(
    n_gx,
    n_gy,
    n_gz,
    cap,
    table,
    volt_in,
    rec_in,
    fiber,
    block_row,
    term_row,
    owner_row,
    tv_in,
    tr_in,
    gain_row,
    cable_row,
    volt_out,
    rec_out,
    tv_out,
    tr_out,
    vp,
    coef,
    into,
    a_mat,
    at_mat,
    tg_mat,
    tgt_mat,
    gain_h,
    gain_o,
    msg_send,
    msg_recv,
    v_send,
    v_recv,
    u_send,
    u_recv,
    hx_send,
    hx_recv,
    hy_send,
    hy_recv,
    msg_sem,
    v_sem_s,
    v_sem_r,
    u_sem_s,
    u_sem_r,
    halo_s,
    halo_r,
):
    gx = lax.axis_index("gx")
    gy = lax.axis_index("gy")
    gz = lax.axis_index("gz")
    n = n_gx * n_gy
    me = gx * n_gy + gy
    depth, rows, width = volt_in.shape
    voxel_rows = depth * rows
    groups = voxel_rows // 8
    per = rows // 8
    slots = n * cap
    terms = tv_in.shape[0]
    jcount = block_row.shape[1]
    shift = cap.bit_length() - 1

    def at_peer(d):
        p = lax.rem(me + d, n)
        return p, {"gx": p // n_gy, "gy": lax.rem(p, n_gy)}

    barrier = pltpu.get_barrier_semaphore()

    def greet(d, carry):
        _, where_to = at_peer(d)
        pl.semaphore_signal(barrier, inc=1, device_id=where_to, device_id_type=MESH)
        return carry

    lax.fori_loop(1, n, greet, 0)

    pl.semaphore_signal(barrier, inc=1, device_id={"gz": n_gz - 1 - gz}, device_id_type=MESH)

    def rows_of(p):
        return pl.ds(pl.multiple_of(p * cap, 8), cap)

    def slot_copy(src, dst, s, d, send_sem, recv_sem):
        p, where_to = at_peer(d)
        return pltpu.make_async_remote_copy(
            src_ref=src.at[s, rows_of(p)],
            dst_ref=dst.at[s, rows_of(me)],
            send_sem=send_sem.at[s],
            recv_sem=recv_sem.at[s],
            device_id=where_to,
            device_id_type=MESH,
        )

    def send_slots(src, dst, s, send_sem, recv_sem):
        def go(d, carry):
            slot_copy(src, dst, s, d, send_sem, recv_sem).start()
            return carry

        lax.fori_loop(1, n, go, 0)
        dst[s, rows_of(me)] = src[s, rows_of(me)]

    def all_slots(src, dst, s, send_sem, recv_sem):
        part = pl.ds(0, (n - 1) * cap)
        _, where_to = at_peer(1)
        return pltpu.make_async_remote_copy(
            src_ref=src.at[s, part],
            dst_ref=dst.at[s, part],
            send_sem=send_sem.at[s],
            recv_sem=recv_sem.at[s],
            device_id=where_to,
            device_id_type=MESH,
        )

    def halo_copies(s):
        def make(src, dst, k, where_to):
            return pltpu.make_async_remote_copy(
                src_ref=src,
                dst_ref=dst,
                send_sem=halo_s.at[s, k],
                recv_sem=halo_r.at[s, k],
                device_id=where_to,
                device_id_type=MESH,
            )

        last = depth + 1
        return (
            (make(vp.at[s, depth], vp.at[s, 0], 0, {"gz": n_gz - 1 - gz}), gz == 0, gz == n_gz - 1),
            (make(vp.at[s, 1], vp.at[s, last], 1, {"gz": n_gz - 1 - gz}), gz == n_gz - 1, gz == 0),
            (make(hx_send.at[s, 1], hx_recv.at[s, 0], 2, {"gx": lax.rem(gx + 1, n_gx)}), gx < n_gx - 1, gx > 0),
            (make(hx_send.at[s, 0], hx_recv.at[s, 1], 3, {"gx": lax.rem(gx + n_gx - 1, n_gx)}), gx > 0, gx < n_gx - 1),
            (make(hy_send.at[s], hy_recv.at[s, 0], 4, {"gy": lax.rem(gy + 1, n_gy)}), gy < n_gy - 1, gy > 0),
            (make(hy_send.at[s], hy_recv.at[s, 1], 5, {"gy": lax.rem(gy + n_gy - 1, n_gy)}), gy > 0, gy < n_gy - 1),
        )

    lane8 = iota((8, width), 1)

    def pack(plane, z, packed):
        for i in range(per):
            k = z * per + i
            piece = plane[i * 8 : i * 8 + 8]
            packed = jnp.where(lane8 == k, piece[:, 0:1], packed)
            packed = jnp.where(lane8 == k + groups, piece[:, width - 1 : width], packed)
        return packed

    def send_halos(s):
        for copy, sends, _ in halo_copies(s):
            pl.when(sends)(copy.start)

        @pl.when(gz == 0)
        def _():
            vp[s, 0] = vp[s, 1]

        @pl.when(gz == n_gz - 1)
        def _():
            vp[s, depth + 1] = vp[s, depth]

    packed = jnp.zeros((8, width), F32)
    for z in range(depth):
        plane = volt_in[z]
        vp[0, z + 1] = plane
        hx_send[0, 0, z : z + 1, :] = plane[0:1]
        hx_send[0, 1, z : z + 1, :] = plane[rows - 1 : rows]
        packed = pack(plane, z, packed)
    hy_send[0] = packed
    rec_out[...] = rec_in[...]
    tv_out[...] = tv_in[...]
    tr_out[...] = tr_in[...]

    owner = jnp.broadcast_to(owner_row[...], (jcount, jcount))
    owner_t = jnp.transpose(owner)
    earlier = (owner_t == owner) & (iota((jcount, jcount), 0) < iota((jcount, jcount), 1))
    rank = jnp.sum(jnp.where(earlier, 1.0, 0.0), axis=0, keepdims=True).astype(jnp.int32)
    slot = owner_row[...] * cap + rank
    holds = iota((slots, jcount), 0) == slot
    holds_b = one_hot(holds)
    tie = one_hot(iota((voxel_rows, jcount), 0) == block_row[...])
    a_mat[...] = dot_nt(holds_b, tie).astype(BF16)
    at_mat[...] = dot_nt(tie, holds_b).astype(BF16)
    term_f = term_row[...].astype(F32) + 1.0
    own_id = jnp.sum(jnp.where(holds, term_f, 0.0), axis=1, keepdims=True)
    slot_lane = iota((slots, 128), 1)
    place = iota((slots, 128), 0) & (cap - 1)
    by_place = jnp.where(slot_lane == place, own_id, 0.0).astype(BF16)
    peer_t = one_hot((iota((n, slots), 1) >> shift) == iota((n, slots), 0))
    ids_out = jnp.dot(peer_t, by_place, preferred_element_type=F32)
    spread = jnp.where(iota((terms, 128), 1) == iota((terms, 128), 0) + GAIN_LANE, 1.0, 0.0)
    gains_lane = jnp.dot(
        jnp.broadcast_to(gain_row[...], (8, terms)), spread, precision=EXACT, preferred_element_type=F32
    )[0:1]
    msg = ids_out + gains_lane
    for p in range(n):
        msg_send[p] = msg[p : p + 1]

    v_send[0] = select_dot(a_mat[...], vp[0, 1 : depth + 1].reshape(voxel_rows, width))

    pl.semaphore_wait(barrier, n)

    def msg_copy(d):
        p, where_to = at_peer(d)
        return pltpu.make_async_remote_copy(
            src_ref=msg_send.at[p],
            dst_ref=msg_recv.at[me],
            send_sem=msg_sem.at[0],
            recv_sem=msg_sem.at[1],
            device_id=where_to,
            device_id_type=MESH,
        )

    def send_msg(d, carry):
        msg_copy(d).start()
        return carry

    lax.fori_loop(1, n, send_msg, 0)
    msg_recv[me] = msg_send[me]
    send_halos(0)
    send_slots(v_send, v_recv, 0, v_sem_s, v_sem_r)

    for z in range(depth):
        klass = fiber[z]
        for k in range(3):
            value = jnp.full(klass.shape, table[k, 0], F32)
            for c in range(1, table.shape[1]):
                value = jnp.where(klass == c, table[k, c], value)
            coef[k, z] = value

    cable = jnp.sum(
        jnp.where(iota((terms, terms), 0) == iota((terms, terms), 1), cable_row[...], 0.0),
        axis=1,
        keepdims=True,
    )

    def all_msgs():
        _, where_to = at_peer(1)
        part = pl.ds(0, n - 1)
        return pltpu.make_async_remote_copy(
            src_ref=msg_send.at[part],
            dst_ref=msg_recv.at[part],
            send_sem=msg_sem.at[0],
            recv_sem=msg_sem.at[1],
            device_id=where_to,
            device_id_type=MESH,
        )

    all_msgs().wait_recv()
    arrived = msg_recv[...].reshape(n, 128)
    peer = jnp.where((iota((slots, n), 0) >> shift) == iota((slots, n), 1), 1.0, 0.0)
    per_slot = jnp.dot(peer, arrived, precision=EXACT, preferred_element_type=F32)
    far_id = jnp.sum(jnp.where(slot_lane == place, per_slot, 0.0), axis=1, keepdims=True)
    far_id = (far_id + 0.5).astype(jnp.int32) - 1
    own_at = (own_id + 0.5).astype(jnp.int32) - 1
    gain_own = jnp.sum(
        jnp.where((slot_lane == own_at + GAIN_LANE) & (own_at >= 0), per_slot, 0.0), axis=1, keepdims=True
    )
    gain_far = jnp.sum(
        jnp.where((slot_lane == far_id + GAIN_LANE) & (far_id >= 0), gains_lane, 0.0), axis=1, keepdims=True
    )
    gain_h[...] = jnp.broadcast_to(gain_own, (slots, width))
    gain_o[...] = jnp.broadcast_to(gain_far, (slots, width))
    tg = one_hot(iota((slots, terms), 1) == far_id)
    tg_mat[...] = tg
    tgt_mat[...] = dot_nt(one_hot(iota((terms, terms), 0) == iota((terms, terms), 1)), tg).astype(BF16)

    u_send[0] = select_dot(tg, tv_out[...])
    send_slots(u_send, u_recv, 0, u_sem_s, u_sem_r)

    row_id = iota((rows, width), 0)
    lane_id = iota((rows, width), 1)

    def step(s, carry):
        for copy, _, receives in halo_copies(s):
            pl.when(receives)(copy.wait_recv)
        all_slots(u_send, u_recv, s, u_sem_s, u_sem_r).wait_recv()
        into[...] = select_dot(at_mat[...], gain_h[...] * (u_recv[s] - v_send[s]))
        mirrored = pltpu.roll(hy_send[s], groups, 1)
        left = jnp.where(gy == 0, mirrored, hy_recv[s, 0])
        right = jnp.where(gy == n_gy - 1, mirrored, hy_recv[s, 1])
        packed = jnp.zeros((8, width), F32)
        for z in range(depth):
            v = vp[s, z + 1]
            w = rec_out[z]
            lap_z = (vp[s, z + 2] + vp[s, z]) - 2.0 * v
            above = jnp.where(gx == n_gx - 1, v[rows - 1 : rows], hx_recv[s, 1, z : z + 1, :])
            below = jnp.where(gx == 0, v[0:1], hx_recv[s, 0, z : z + 1, :])
            up = jnp.where(row_id == rows - 1, above, pltpu.roll(v, rows - 1, 0))
            down = jnp.where(row_id == 0, below, pltpu.roll(v, 1, 0))
            lap_x = (up + down) - 2.0 * v
            k = z * per
            low = jnp.concatenate([left[:, groups + k + i : groups + k + i + 1] for i in range(per)], axis=0)
            high = jnp.concatenate([right[:, k + i : k + i + 1] for i in range(per)], axis=0)
            before = jnp.where(lane_id == 0, low, pltpu.roll(v, 1, 1))
            after = jnp.where(lane_id == width - 1, high, pltpu.roll(v, width - 1, 1))
            lap_y = (before + after) - 2.0 * v
            react = -8.0 * v * (v - 0.15) * (v - 1.0) - v * w
            drive = into[z * rows : (z + 1) * rows]
            new_v = v + (coef[0, z] * lap_z + coef[1, z] * lap_x + coef[2, z] * lap_y) + 0.1 * (react + drive)
            rec_out[z] = w + 0.01 * (-w - 8.0 * v * (v - 1.15))
            vp[s + 1, z + 1] = new_v
            hx_send[s + 1, 0, z : z + 1, :] = new_v[0:1]
            hx_send[s + 1, 1, z : z + 1, :] = new_v[rows - 1 : rows]
            packed = pack(new_v, z, packed)
        hy_send[s + 1] = packed

        @pl.when(s < STEPS - 1)
        def _():
            send_halos(s + 1)
            v_send[s + 1] = select_dot(a_mat[...], vp[s + 1, 1 : depth + 1].reshape(voxel_rows, width))
            send_slots(v_send, v_recv, s + 1, v_sem_s, v_sem_r)

        all_slots(v_send, v_recv, s, v_sem_s, v_sem_r).wait_recv()
        into_term = select_dot(tgt_mat[...], gain_o[...] * (v_recv[s] - u_send[s]))
        u = tv_out[...]
        r = tr_out[...]
        ends = iota(u.shape, 1)
        before = jnp.where(ends == 0, u, pltpu.roll(u, 1, 1))
        after = jnp.where(ends == width - 1, u, pltpu.roll(u, width - 1, 1))
        lap_k = (before + after) - 2.0 * u
        react = -8.0 * u * (u - 0.15) * (u - 1.0) - u * r
        new_u = u + cable * lap_k + 0.1 * (react + 0.1 * into_term)
        tr_out[...] = r + 0.01 * (-r - 8.0 * u * (u - 1.15))
        tv_out[...] = new_u

        @pl.when(s < STEPS - 1)
        def _():
            u_send[s + 1] = select_dot(tg_mat[...], new_u)
            send_slots(u_send, u_recv, s + 1, u_sem_s, u_sem_r)

        return carry

    lax.fori_loop(0, STEPS, step, 0)
    volt_out[...] = vp[STEPS, 1 : depth + 1]

    all_msgs().wait_send()

    def finish(s, carry):
        for copy, sends, _ in halo_copies(s):
            pl.when(sends)(copy.wait_send)
        all_slots(v_send, v_recv, s, v_sem_s, v_sem_r).wait_send()
        all_slots(u_send, u_recv, s, u_sem_s, u_sem_r).wait_send()
        return carry

    lax.fori_loop(0, STEPS, finish, 0)


def on_device(sizes, volt, recovery, fiber_class, fiber_table, junction_block, junction_term, junction_owner, term_volt, term_recovery, term_gain, cable_gain):
    n_gx, n_gy, n_gz = sizes
    depth, rows, width = volt.shape
    n = n_gx * n_gy
    jcount = junction_block.shape[0]
    terms = term_volt.shape[0]
    most = max(8, 2 * jcount // n)
    cap = 1 << (most - 1).bit_length()
    slots = n * cap
    voxel_rows = depth * rows
    vmem = pl.BlockSpec(memory_space=pltpu.VMEM)
    smem = pl.BlockSpec(memory_space=pltpu.SMEM)
    dma = pltpu.SemaphoreType.DMA
    return pl.pallas_call(
        functools.partial(kernel, n_gx, n_gy, n_gz, cap),
        out_shape=(
            jax.ShapeDtypeStruct(volt.shape, F32),
            jax.ShapeDtypeStruct(volt.shape, F32),
            jax.ShapeDtypeStruct(term_volt.shape, F32),
            jax.ShapeDtypeStruct(term_volt.shape, F32),
        ),
        in_specs=[smem] + [vmem] * 10,
        out_specs=(vmem,) * 4,
        scratch_shapes=[
            pltpu.VMEM((STEPS + 1, depth + 2, rows, width), F32),
            pltpu.VMEM((3, depth, rows, width), F32),
            pltpu.VMEM((voxel_rows, width), F32),
            pltpu.VMEM((slots, voxel_rows), BF16),
            pltpu.VMEM((voxel_rows, slots), BF16),
            pltpu.VMEM((slots, terms), BF16),
            pltpu.VMEM((terms, slots), BF16),
            pltpu.VMEM((slots, width), F32),
            pltpu.VMEM((slots, width), F32),
            pltpu.VMEM((n, 1, 128), F32),
            pltpu.VMEM((n, 1, 128), F32),
            pltpu.VMEM((STEPS, slots, width), F32),
            pltpu.VMEM((STEPS, slots, width), F32),
            pltpu.VMEM((STEPS, slots, width), F32),
            pltpu.VMEM((STEPS, slots, width), F32),
            pltpu.VMEM((STEPS + 1, 2, depth, width), F32),
            pltpu.VMEM((STEPS, 2, depth, width), F32),
            pltpu.VMEM((STEPS + 1, 8, width), F32),
            pltpu.VMEM((STEPS, 2, 8, width), F32),
            dma((2,)),
            dma((STEPS,)),
            dma((STEPS,)),
            dma((STEPS,)),
            dma((STEPS,)),
            dma((STEPS, 6)),
            dma((STEPS, 6)),
        ],
        compiler_params=pltpu.CompilerParams(
            collective_id=0, has_side_effects=True, vmem_limit_bytes=48 * 1024 * 1024
        ),
        name="slab",
    )(
        fiber_table,
        volt,
        recovery,
        fiber_class,
        junction_block.reshape(1, jcount),
        junction_term.reshape(1, jcount),
        junction_owner.reshape(1, jcount),
        term_volt,
        term_recovery,
        term_gain.reshape(1, terms),
        cable_gain.reshape(1, terms),
    )


def solution(mesh):
    sizes = (mesh.shape["gx"], mesh.shape["gy"], mesh.shape["gz"])
    return jax.shard_map(
        functools.partial(on_device, sizes),
        mesh=mesh,
        in_specs=(
            P("gz", "gx", "gy"),
            P("gz", "gx", "gy"),
            P("gz", "gx", "gy"),
            P(),
            P(("gx", "gy", "gz")),
            P(("gx", "gy", "gz")),
            P(("gx", "gy", "gz"), None),
            P(("gx", "gy", "gz"), None),
            P(("gx", "gy", "gz"), None),
            P(("gx", "gy", "gz")),
            P(("gx", "gy", "gz")),
        ),
        out_specs=(
            P("gz", "gx", "gy"),
            P("gz", "gx", "gy"),
            P(("gx", "gy", "gz"), None),
            P(("gx", "gy", "gz"), None),
        ),
        check_vma=False,
    )
```

time: 293 us -> 50.2 us (0.17)
  starting transfers between devices: 90.7 us -> 0 us
  waiting for transfers between devices: 89.9 us -> 0 us
  other arithmetic: 79.3 us -> 0 us
  Pallas kernels: 0 us -> 41.6 us
  local copies, waits for them, and re-layouts: 28.3 us -> 7.58 us
    ppermute x24 -> x0, waiting for transfers between devices: 48.9 us -> none  [the longest x12 40.2 us: extended(): lax.ppermute(head, axis, [((i + 1) % count, i) for i in range(ends)])]
    all_to_all x9 -> x0, starting transfers between devices: 45.4 us -> none  [the longest x4 19 us: on_device(): lax.all_to_all(current, ('gx', 'gy'), split_axis=0, concat_axis=0, tiled=...]
    ppermute x24 -> x0, starting transfers between devices: 45.3 us -> none  [the longest x12 29.8 us: extended(): lax.ppermute(tail, axis, [(i, (i + 1) % count) for i in range(ends)])]
    pallas_call x0 -> x1, Pallas kernels: none -> 41.6 us  [on_device(): pl.pallas_call(functools.partial(kernel, n_gx, n_gy, n_gz, cap), out_shap...]
    all_to_all x9 -> x0, waiting for transfers between devices: 41 us -> none  [the longest x4 24.4 us: on_device(): lax.all_to_all(current, ('gx', 'gy'), split_axis=0, concat_axis=0, tiled=...]
    select_n x25 -> x0, other arithmetic: 27.7 us -> none  [the longest x2 20.5 us: on_device(): gains = jnp.where(valid, term_gain[safe_ids], 0.0)]
    add x8 -> x0, other arithmetic: 27.1 us -> none  [the longest x3 22.4 us: on_device(): new_v = volt + (coef_z * lap_z + coef_x * lap_x + coef_y * lap_y) + react_v]
    scatter-add x8 -> x0, other arithmetic: 15.2 us -> none  [the longest x4 8.19 us: on_device(): jax.ops.segment_sum(returned[slot], junction_block, num_segments=depth *...]
  transfers between devices with their start and end apart: 33 -> 0, of which waited for: 18 -> 0; matrix products, arithmetic and copies ran while one was open for 21% -> 0% of each run, Pallas kernels for 0% -> 0%
where the time goes in v1:
time: 50.2 us; the launch traced here: 49.9 us
  Pallas kernels  41.6 us (83%)
  local copies, waits for them, and re-layouts  7.58 us (15%)
  between operations  0.7 us (1%)
    pallas_call x1, Pallas kernels, on_device(): pl.pallas_call(functools.partial(kernel, n_gx, n_gy, n_gz, cap), out_shap...  41.6 us
    unnamed x26, local copies, waits for them, and re-layouts  7.58 us

profile of v1, /device:TPU:0, one launch (start us, length us, event | category | flops | bytes accessed | tf_op | source)
XLA Modules:
  0.0 49.9 jit_solution(12982502926396083296)
XLA Ops:
  0.6 0.0 copy-start.9
  0.6 0.0 copy-start.10
  0.7 0.0 copy-start.5
  0.7 0.0 copy-start.6
  0.7 0.0 copy-start.7
  0.7 0.0 copy-start.8
  0.7 0.6 %copy-done.9 = f32[32]{0:T(128)S(1)} copy-done((f32[32]{0:T(128)S(1)}, f32[32]{0:T(128)}, u32[]{:S(2)}) %copy-start.9) | copy-done | bytes 152
  1.3 0.0 copy-done.10
  1.3 0.0 copy-done.5
  1.3 0.0 copy-done.6
  1.4 0.0 copy-done.7
  1.4 0.0 copy-done.8
  1.4 0.0 copy-start
  1.4 0.9 %copy-done = f32[16,32,128]{2,1,0:T(8,128)S(1)} copy-done((f32[16,32,128]{2,1,0:T(8,128)S(1)}, f32[16,32,128]{2,1,0:T(8,128)}, u32[]{:S(2)}) %copy-start) | copy-done | bytes 262168
  2.3 0.0 copy-start.1
  2.3 0.9 %copy-done.1 = f32[16,32,128]{2,1,0:T(8,128)S(1)} copy-done((f32[16,32,128]{2,1,0:T(8,128)S(1)}, f32[16,32,128]{2,1,0:T(8,128)}, u32[]{:S(2)}) %copy-start.1) | copy-done | bytes 262168
  3.3 0.0 copy-start.2
  3.3 0.9 %copy-done.2 = s32[16,32,128]{2,1,0:T(8,128)S(1)} copy-done((s32[16,32,128]{2,1,0:T(8,128)S(1)}, s32[16,32,128]{2,1,0:T(8,128)}, u32[]{:S(2)}) %copy-start.2) | copy-done | bytes 262168
  4.2 0.0 copy-start.3
  4.2 0.7 %copy-done.3 = f32[32,128]{1,0:T(8,128)S(1)} copy-done((f32[32,128]{1,0:T(8,128)S(1)}, f32[32,128]{1,0:T(8,128)}, u32[]{:S(2)}) %copy-start.3) | copy-done | bytes 16408
  4.9 0.0 copy-start.4
  4.9 0.7 %copy-done.4 = f32[32,128]{1,0:T(8,128)S(1)} copy-done((f32[32,128]{1,0:T(8,128)S(1)}, f32[32,128]{1,0:T(8,128)}, u32[]{:S(2)}) %copy-start.4) | copy-done | bytes 16408
  5.7 41.6 %slab.1 = (f32[16,32,128]{2,1,0:T(8,128)S(1)}, f32[16,32,128]{2,1,0:T(8,128)S(1)}, f32[32,128]{1,0:T(8,128)S(1)}, f32[32,128]{1,0:T(8,128)S(1)}) custom-call(f32[3,8]{1,0:T(4,128)S(1)} %copy-done.5, f32[16,32,128]{2,1,0:T(8,128)S(1)} %copy-done, f32[16,32,128]{2,1,0:T(8,128)S(1)} %copy-done.1, s32[16,32,128]{2,1,0:T(8,128)S(1)} %copy-done.2, ...), custom_call_target="tpu_custom_call" | custom-call | tf_op jit(solution)/shard_map/slab/pallas_call | solution.py:393
  47.3 0.7 %copy.19 = f32[16,32,128]{2,1,0:T(8,128)} copy(f32[16,32,128]{2,1,0:T(8,128)S(1)} %get-tuple-element.8) | data formatting | bytes 524288
  48.0 0.7 %copy.20 = f32[16,32,128]{2,1,0:T(8,128)} copy(f32[16,32,128]{2,1,0:T(8,128)S(1)} %get-tuple-element.9) | data formatting | bytes 524288
  48.7 0.6 %copy.21 = f32[32,128]{1,0:T(8,128)} copy(f32[32,128]{1,0:T(8,128)S(1)} %get-tuple-element.10) | data formatting | bytes 32768
  49.3 0.6 %copy.22 = f32[32,128]{1,0:T(8,128)} copy(f32[32,128]{1,0:T(8,128)S(1)} %get-tuple-element.11) | data formatting | bytes 32768
Async XLA Ops:
  0.6 0.7 %copy-start.9 = (f32[32]{0:T(128)S(1)}, f32[32]{0:T(128)}, u32[]{:S(2)}) copy-start(f32[32]{0:T(128)} %param.20) | copy-start | bytes 388
  0.6 0.7 %copy-start.10 = (f32[32]{0:T(128)S(1)}, f32[32]{0:T(128)}, u32[]{:S(2)}) copy-start(f32[32]{0:T(128)} %param.21) | copy-start | bytes 388
  0.7 0.7 %copy-start.5 = (f32[3,8]{1,0:T(4,128)S(1)}, f32[3,8]{1,0:T(4,128)}, u32[]{:S(2)}) copy-start(f32[3,8]{1,0:T(4,128)} %table.1) | copy-start | bytes 292
  0.7 0.7 %copy-start.6 = (s32[128]{0:T(128)S(1)}, s32[128]{0:T(128)}, u32[]{:S(2)}) copy-start(s32[128]{0:T(128)} %param.15) | copy-start | bytes 1540
  0.7 0.7 %copy-start.7 = (s32[128]{0:T(128)S(1)}, s32[128]{0:T(128)}, u32[]{:S(2)}) copy-start(s32[128]{0:T(128)} %param.16) | copy-start | bytes 1540
  0.7 0.7 %copy-start.8 = (s32[128,1]{0,1:T(1,128)S(1)}, s32[128,1]{0,1:T(1,128)}, u32[]{:S(2)}) copy-start(s32[128,1]{0,1:T(1,128)} %param.17) | copy-start | bytes 1540
  1.4 0.9 %copy-start = (f32[16,32,128]{2,1,0:T(8,128)S(1)}, f32[16,32,128]{2,1,0:T(8,128)}, u32[]{:S(2)}) copy-start(f32[16,32,128]{2,1,0:T(8,128)} %volt_in.1) | copy-start | bytes 786436
  2.3 0.9 %copy-start.1 = (f32[16,32,128]{2,1,0:T(8,128)S(1)}, f32[16,32,128]{2,1,0:T(8,128)}, u32[]{:S(2)}) copy-start(f32[16,32,128]{2,1,0:T(8,128)} %rec_in.1) | copy-start | bytes 786436
  3.3 0.9 %copy-start.2 = (s32[16,32,128]{2,1,0:T(8,128)S(1)}, s32[16,32,128]{2,1,0:T(8,128)}, u32[]{:S(2)}) copy-start(s32[16,32,128]{2,1,0:T(8,128)} %fiber.1) | copy-start | bytes 786436
  4.2 0.7 %copy-start.3 = (f32[32,128]{1,0:T(8,128)S(1)}, f32[32,128]{1,0:T(8,128)}, u32[]{:S(2)}) copy-start(f32[32,128]{1,0:T(8,128)} %tv_in.1) | copy-start | bytes 49156
  4.9 0.7 %copy-start.4 = (f32[32,128]{1,0:T(8,128)S(1)}, f32[32,128]{1,0:T(8,128)}, u32[]{:S(2)}) copy-start(f32[32,128]{1,0:T(8,128)} %tr_in.1) | copy-start | bytes 49156

commit v2 on v1

--- a/solution.py
+++ b/solution.py
@@ -60,6 +60,10 @@
     vp,
     coef,
     into,
+    klasses,
+    same_mat,
+    v_base,
+    current,
     a_mat,
     at_mat,
     tg_mat,
@@ -83,6 +87,7 @@
     u_sem_r,
     halo_s,
     halo_r,
+    in_sem,
 ):
     gx = lax.axis_index("gx")
     gy = lax.axis_index("gy")
@@ -102,6 +107,19 @@
         p = lax.rem(me + d, n)
         return p, {"gx": p // n_gy, "gy": lax.rem(p, n_gy)}
 
+    loads = [
+        pltpu.make_async_copy(src, dst, in_sem.at[k])
+        for k, (src, dst) in enumerate(
+            (
+                (volt_in, vp.at[0, pl.ds(1, depth)]),
+                (fiber, klasses),
+                (tv_in, tv_out),
+                (tr_in, tr_out),
+                (rec_in, rec_out),
+            )
+        )
+    ]
+
     barrier = pltpu.get_barrier_semaphore()
 
     def greet(d, carry):
@@ -112,6 +130,9 @@
     lax.fori_loop(1, n, greet, 0)
 
     pl.semaphore_signal(barrier, inc=1, device_id={"gz": n_gz - 1 - gz}, device_id_type=MESH)
+
+    for load in loads:
+        load.start()
 
     def rows_of(p):
         return pl.ds(pl.multiple_of(p * cap, 8), cap)
@@ -189,18 +210,6 @@
         @pl.when(gz == n_gz - 1)
         def _():
             vp[s, depth + 1] = vp[s, depth]
-
-    packed = jnp.zeros((8, width), F32)
-    for z in range(depth):
-        plane = volt_in[z]
-        vp[0, z + 1] = plane
-        hx_send[0, 0, z : z + 1, :] = plane[0:1]
-        hx_send[0, 1, z : z + 1, :] = plane[rows - 1 : rows]
-        packed = pack(plane, z, packed)
-    hy_send[0] = packed
-    rec_out[...] = rec_in[...]
-    tv_out[...] = tv_in[...]
-    tr_out[...] = tr_in[...]
 
     owner = jnp.broadcast_to(owner_row[...], (jcount, jcount))
     owner_t = jnp.transpose(owner)
@@ -227,6 +236,14 @@
     for p in range(n):
         msg_send[p] = msg[p : p + 1]
 
+    loads[0].wait()
+    packed = jnp.zeros((8, width), F32)
+    for z in range(depth):
+        plane = vp[0, z + 1]
+        hx_send[0, 0, z : z + 1, :] = plane[0:1]
+        hx_send[0, 1, z : z + 1, :] = plane[rows - 1 : rows]
+        packed = pack(plane, z, packed)
+    hy_send[0] = packed
     v_send[0] = select_dot(a_mat[...], vp[0, 1 : depth + 1].reshape(voxel_rows, width))
 
     pl.semaphore_wait(barrier, n)
@@ -251,8 +268,9 @@
     send_halos(0)
     send_slots(v_send, v_recv, 0, v_sem_s, v_sem_r)
 
+    loads[1].wait()
     for z in range(depth):
-        klass = fiber[z]
+        klass = klasses[z]
         for k in range(3):
             value = jnp.full(klass.shape, table[k, 0], F32)
             for c in range(1, table.shape[1]):
@@ -296,21 +314,22 @@
     tg_mat[...] = tg
     tgt_mat[...] = dot_nt(one_hot(iota((terms, terms), 0) == iota((terms, terms), 1)), tg).astype(BF16)
 
+    loads[2].wait()
     u_send[0] = select_dot(tg, tv_out[...])
     send_slots(u_send, u_recv, 0, u_sem_s, u_sem_r)
 
+    same_mat[...] = dot_nt(a_mat[...], a_mat[...]).astype(BF16)
+    loads[3].wait()
+    loads[4].wait()
     row_id = iota((rows, width), 0)
     lane_id = iota((rows, width), 1)
 
-    def step(s, carry):
+    def base(s):
         for copy, _, receives in halo_copies(s):
             pl.when(receives)(copy.wait_recv)
-        all_slots(u_send, u_recv, s, u_sem_s, u_sem_r).wait_recv()
-        into[...] = select_dot(at_mat[...], gain_h[...] * (u_recv[s] - v_send[s]))
         mirrored = pltpu.roll(hy_send[s], groups, 1)
         left = jnp.where(gy == 0, mirrored, hy_recv[s, 0])
         right = jnp.where(gy == n_gy - 1, mirrored, hy_recv[s, 1])
-        packed = jnp.zeros((8, width), F32)
         for z in range(depth):
             v = vp[s, z + 1]
             w = rec_out[z]
@@ -327,9 +346,27 @@
             after = jnp.where(lane_id == width - 1, high, pltpu.roll(v, width - 1, 1))
             lap_y = (before + after) - 2.0 * v
             react = -8.0 * v * (v - 0.15) * (v - 1.0) - v * w
-            drive = into[z * rows : (z + 1) * rows]
-            new_v = v + (coef[0, z] * lap_z + coef[1, z] * lap_x + coef[2, z] * lap_y) + 0.1 * (react + drive)
+            vp[s + 1, z + 1] = v + (coef[0, z] * lap_z + coef[1, z] * lap_x + coef[2, z] * lap_y) + 0.1 * react
             rec_out[z] = w + 0.01 * (-w - 8.0 * v * (v - 1.15))
+
+        @pl.when(s < STEPS - 1)
+        def _():
+            v_base[...] = select_dot(a_mat[...], vp[s + 1, 1 : depth + 1].reshape(voxel_rows, width))
+
+    def currents(s):
+        all_slots(u_send, u_recv, s, u_sem_s, u_sem_r).wait_recv()
+        current[...] = gain_h[...] * (u_recv[s] - v_send[s])
+
+        @pl.when(s < STEPS - 1)
+        def _():
+            v_send[s + 1] = v_base[...] + 0.1 * select_dot(same_mat[...], current[...])
+            send_slots(v_send, v_recv, s + 1, v_sem_s, v_sem_r)
+
+    def voxels(s):
+        into[...] = select_dot(at_mat[...], current[...])
+        packed = jnp.zeros((8, width), F32)
+        for z in range(depth):
+            new_v = vp[s + 1, z + 1] + 0.1 * into[z * rows : (z + 1) * rows]
             vp[s + 1, z + 1] = new_v
             hx_send[s + 1, 0, z : z + 1, :] = new_v[0:1]
             hx_send[s + 1, 1, z : z + 1, :] = new_v[rows - 1 : rows]
@@ -339,9 +376,8 @@
         @pl.when(s < STEPS - 1)
         def _():
             send_halos(s + 1)
-            v_send[s + 1] = select_dot(a_mat[...], vp[s + 1, 1 : depth + 1].reshape(voxel_rows, width))
-            send_slots(v_send, v_recv, s + 1, v_sem_s, v_sem_r)
-
+
+    def terminals(s):
         all_slots(v_send, v_recv, s, v_sem_s, v_sem_r).wait_recv()
         into_term = select_dot(tgt_mat[...], gain_o[...] * (v_recv[s] - u_send[s]))
         u = tv_out[...]
@@ -360,9 +396,19 @@
             u_send[s + 1] = select_dot(tg_mat[...], new_u)
             send_slots(u_send, u_recv, s + 1, u_sem_s, u_sem_r)
 
+    def two_steps(i, carry):
+        s = 2 * i
+        base(s)
+        terminals(s)
+        currents(s)
+        voxels(s)
+        base(s + 1)
+        currents(s + 1)
+        voxels(s + 1)
+        terminals(s + 1)
         return carry
 
-    lax.fori_loop(0, STEPS, step, 0)
+    lax.fori_loop(0, STEPS // 2, two_steps, 0)
     volt_out[...] = vp[STEPS, 1 : depth + 1]
 
     all_msgs().wait_send()
@@ -388,6 +434,7 @@
     slots = n * cap
     voxel_rows = depth * rows
     vmem = pl.BlockSpec(memory_space=pltpu.VMEM)
+    hbm = pl.BlockSpec(memory_space=pltpu.HBM)
     smem = pl.BlockSpec(memory_space=pltpu.SMEM)
     dma = pltpu.SemaphoreType.DMA
     return pl.pallas_call(
@@ -398,12 +445,16 @@
             jax.ShapeDtypeStruct(term_volt.shape, F32),
             jax.ShapeDtypeStruct(term_volt.shape, F32),
         ),
-        in_specs=[smem] + [vmem] * 10,
+        in_specs=[smem] + [hbm] * 3 + [vmem] * 3 + [hbm] * 2 + [vmem] * 2,
         out_specs=(vmem,) * 4,
         scratch_shapes=[
             pltpu.VMEM((STEPS + 1, depth + 2, rows, width), F32),
             pltpu.VMEM((3, depth, rows, width), F32),
             pltpu.VMEM((voxel_rows, width), F32),
+            pltpu.VMEM((depth, rows, width), jnp.int32),
+            pltpu.VMEM((slots, slots), BF16),
+            pltpu.VMEM((slots, width), F32),
+            pltpu.VMEM((slots, width), F32),
             pltpu.VMEM((slots, voxel_rows), BF16),
             pltpu.VMEM((voxel_rows, slots), BF16),
             pltpu.VMEM((slots, terms), BF16),
@@ -427,9 +478,10 @@
             dma((STEPS,)),
             dma((STEPS, 6)),
             dma((STEPS, 6)),
+            dma((5,)),
         ],
         compiler_params=pltpu.CompilerParams(
-            collective_id=0, has_side_effects=True, vmem_limit_bytes=48 * 1024 * 1024
+            collective_id=0, has_side_effects=True, vmem_limit_bytes=64 * 1024 * 1024 - 65536
         ),
         name="slab",
     )(

time: 50.2 us -> 43.4 us (0.86)
  local copies, waits for them, and re-layouts: 7.58 us -> 3.76 us
  Pallas kernels: 41.6 us -> 38.6 us
    unnamed x26 -> x10, local copies, waits for them, and re-layouts: 7.58 us -> 3.76 us
    pallas_call x1, Pallas kernels: 41.6 us -> 38.6 us  [on_device(): pl.pallas_call(functools.partial(kernel, n_gx, n_gy, n_gz, cap), out_shap...]
where the time goes in v2:
time: 43.4 us; the launch traced here: 43.1 us
  Pallas kernels  38.6 us (89%)
  local copies, waits for them, and re-layouts  3.76 us (9%)
  between operations  0.66 us (2%)
    pallas_call x1, Pallas kernels, on_device(): pl.pallas_call(functools.partial(kernel, n_gx, n_gy, n_gz, cap), out_shap...  38.6 us
    unnamed x10, local copies, waits for them, and re-layouts  3.76 us

profile of v2, /device:TPU:0, one launch (start us, length us, event | category | flops | bytes accessed | tf_op | source)
XLA Modules:
  0.0 43.1 jit_solution(9069456881828118831)
XLA Ops:
  0.6 38.6 %slab.1 = (f32[16,32,128]{2,1,0:T(8,128)}, f32[16,32,128]{2,1,0:T(8,128)}, f32[32,128]{1,0:T(8,128)}, f32[32,128]{1,0:T(8,128)}) custom-call(f32[3,8]{1,0:T(4,128)} %table.1, f32[16,32,128]{2,1,0:T(8,128)} %volt_in.1, f32[16,32,128]{2,1,0:T(8,128)} %rec_in.1, s32[16,32,128]{2,1,0:T(8,128)} %fiber.1, s32[1,128]{1,0:T(1,128)} %bitcast.5, s32[1,128]{1,0:T(1,128)} %bitcast.6, ...), custom_call_target="tpu_custom_call" | custom-call | tf_op jit(solution)/shard_map/slab/pallas_call | solution.py:440
  39.3 0.0 copy-start
  39.3 1.7 %copy.19 = f32[16,32,128]{2,1,0:T(8,128)} copy(f32[16,32,128]{2,1,0:T(8,128)} %get-tuple-element.8) | data formatting | bytes 524288
  41.0 0.0 copy-done
  41.0 0.0 copy-start.2
  41.0 0.7 %copy.20 = f32[16,32,128]{2,1,0:T(8,128)} copy(f32[16,32,128]{2,1,0:T(8,128)S(1)} %copy-done) | data formatting | bytes 524288
  41.7 0.0 copy-done.2
  41.7 0.0 copy-start.1
  41.7 0.6 %copy.21 = f32[32,128]{1,0:T(8,128)} copy(f32[32,128]{1,0:T(8,128)S(1)} %copy-done.2) | data formatting | bytes 32768
  42.3 0.1 copy-done.1
  42.4 0.6 %copy.22 = f32[32,128]{1,0:T(8,128)} copy(f32[32,128]{1,0:T(8,128)S(1)} %copy-done.1) | data formatting | bytes 32768
Async XLA Ops:
  39.3 1.7 %copy-start = (f32[16,32,128]{2,1,0:T(8,128)S(1)}, f32[16,32,128]{2,1,0:T(8,128)}, u32[]{:S(2)}) copy-start(f32[16,32,128]{2,1,0:T(8,128)} %get-tuple-element.9) | copy-start | bytes 786436
  41.0 0.7 %copy-start.2 = (f32[32,128]{1,0:T(8,128)S(1)}, f32[32,128]{1,0:T(8,128)}, u32[]{:S(2)}) copy-start(f32[32,128]{1,0:T(8,128)} %get-tuple-element.10) | copy-start | bytes 49156
  41.7 0.7 %copy-start.1 = (f32[32,128]{1,0:T(8,128)S(1)}, f32[32,128]{1,0:T(8,128)}, u32[]{:S(2)}) copy-start(f32[32,128]{1,0:T(8,128)} %get-tuple-element.11) | copy-start | bytes 49156
